TPU v7x, 128 devices: a whole 4x4x4 slice. The times are simulated.
128 devices in a mesh: row: 8 (over x_lo, y), col: 16 (over z, x_hi, core).
Axes of the slice: x: 4 (x_hi: 2, x_lo: 2; x = x_hi * 2 + x_lo), y: 4, z: 4, core: 2. Of those that a mesh axis runs over, the one named last changes fastest.
Arguments:
- cells: bfloat16 [512, 512, 256], P('row', 'col'), may hold values from -20 to 20
- row_gain: float32 [256], replicated, may hold values from 0.1 to 1.9
- row_qk: bfloat16 [256, 512], replicated, may hold values from -30 to 30
- row_value: bfloat16 [256, 256], replicated, may hold values from -0.375 to 0.375
- row_out: bfloat16 [256, 256], replicated, may hold values from -0.375 to 0.375
- col_gain: float32 [256], replicated, may hold values from 0.1 to 1.9
- col_qk: bfloat16 [256, 512], replicated, may hold values from -30 to 30
- col_value: bfloat16 [256, 256], replicated, may hold values from -0.375 to 0.375
- col_out: bfloat16 [256, 256], replicated, may hold values from -0.375 to 0.375
- mlp_gain: float32 [256], replicated, may hold values from 0.1 to 1.9
- mlp_in: bfloat16 [256, 1024], replicated, may hold values from -0.375 to 0.375
- mlp_out: bfloat16 [1024, 256], replicated, may hold values from -0.1875 to 0.1875
Outputs:
- result: bfloat16 [512, 512, 256], P('row', 'col')
All inputs are finite; a program needn't handle non-finite values.
Results may differ from a plain program's by a relative error of at most 0.012.
Values may be sent and summed in bfloat16 or wider, within the bound.
No kernel may reach another device: no remote copies, remote signals or barrier semaphores. Data moves between devices by JAX's collectives and lax.ppermute only.
A program may use at most 64 MiB of HBM per device.

v0:
```python
import functools
import math

import jax
import jax.numpy as jnp
from jax import lax
from jax.experimental import pallas as pl
from jax.experimental.pallas import tpu as pltpu
from jax.sharding import PartitionSpec as P

HEADS = 8
HEAD = 32
WIDTH = 256
LINE = 512
LINES = 4
HALF = 128
GROUPS = 2
IN_GROUP = 4
BLOCK = 256
CHUNK = 256
LEAST, MOST = 2.0**-60, 2.0**100
SCALE = math.log2(math.e) / math.sqrt(HEAD)
GELU_A = math.sqrt(2.0 / math.pi)
GELU_B = GELU_A * 0.044715


def layer_norm(values, gain):
    mean = jnp.mean(values, axis=-1, keepdims=True)
    centred = values - mean
    variance = jnp.mean(centred * centred, axis=-1, keepdims=True)
    return centred * lax.rsqrt(variance + 1e-05) * gain


def matmul(left, right):
    return jnp.dot(left, right, preferred_element_type=jnp.float32)


def dot(left, right, left_dim, right_dim):
    return lax.dot_general(
        left, right, (((left_dim,), (right_dim,)), ((), ())), preferred_element_type=jnp.float32
    )


class Line:
    def __init__(self, shift, load, store, gain, qk_w, val_w, out_w, probs):
        self.shift = shift
        self.load, self.store = load, store
        self.gain, self.qk_w, self.val_w, self.out_w = gain, qk_w, val_w, out_w
        self.probs = probs
        self.chunk = CHUNK if shift else LINE
        self.largest = {}
        self.mixed = []
        self.fits = []

    def project(self):
        normed = layer_norm(self.load(), self.gain[...]).astype(jnp.bfloat16)
        both = matmul(normed, self.qk_w[...])
        self.values = dot(self.val_w[...], normed, 0, 1).astype(jnp.bfloat16)
        query = both[:, :WIDTH].astype(jnp.bfloat16).astype(jnp.float32) * SCALE
        self.query_hi = query.astype(jnp.bfloat16)
        self.query_lo = (query - self.query_hi.astype(jnp.float32)).astype(jnp.bfloat16)
        self.keys = both[:, WIDTH:].astype(jnp.bfloat16)

    def weigh(self, group):
        lanes = slice(group * HALF, (group + 1) * HALF)
        query = jnp.concatenate([self.query_hi[:, lanes], self.query_lo[:, lanes]], axis=1)
        keys = self.keys[:, lanes]
        zero = jnp.zeros_like(keys)
        lane = lax.broadcasted_iota(jnp.int32, (LINE, HALF), 1) // HEAD
        for head in range(IN_GROUP):
            head_keys = jnp.where(lane == head, keys, zero)
            head_keys = jnp.concatenate([head_keys, head_keys], axis=1)
            for start in range(0, LINE, BLOCK):
                here = slice(start, start + BLOCK)
                for chunk in range(0, LINE, self.chunk):
                    rows = slice(chunk, chunk + self.chunk)
                    scores = dot(head_keys[rows], query[here], 1, 1)
                    if self.shift:
                        largest = jnp.max(scores, axis=0, keepdims=True)
                        self.largest[group, head, chunk, start] = largest
                        scores = scores - largest
                    weights = jnp.exp2(scores).astype(jnp.bfloat16)
                    self.probs[group * IN_GROUP + head, rows, here] = weights

    def mix(self, group):
        ones = jnp.ones((16, LINE), jnp.bfloat16)
        for head in range(IN_GROUP):
            index = group * IN_GROUP + head
            values = jnp.concatenate([self.values[index * HEAD : (index + 1) * HEAD], ones], axis=0)
            if self.shift:
                total = self.sum_chunks(group, head, values)
            else:
                total = matmul(values, self.probs[index])
                weight = total[HEAD : HEAD + 1]
                fits = (weight >= LEAST) & (weight <= MOST)
                self.fits.append(jnp.where(fits, 1.0, 0.0))
            self.mixed.append((total[:HEAD] / total[HEAD : HEAD + 1]).astype(jnp.bfloat16))

    def sum_chunks(self, group, head, values):
        chunks = range(0, LINE, self.chunk)
        scales = [
            jnp.concatenate(
                [self.largest[group, head, chunk, start] for start in range(0, LINE, BLOCK)], axis=1
            )
            for chunk in chunks
        ]
        largest = functools.reduce(jnp.maximum, scales)
        total = 0.0
        for chunk, scale in zip(chunks, scales):
            rows = slice(chunk, chunk + self.chunk)
            part = matmul(values[:, rows], self.probs[group * IN_GROUP + head, rows])
            total += part * jnp.exp2(scale - largest)
        return total

    def finish(self):
        self.store(self.load() + dot(jnp.concatenate(self.mixed, axis=0), self.out_w[...], 0, 0))


def run(lines):
    lines[0].project()
    lines[0].weigh(0)
    for line, later in zip(lines, lines[1:] + [None]):
        line.mix(0)
        line.weigh(1)
        if later is not None:
            later.project()
        line.mix(1)
        if later is not None:
            later.weigh(0)
        line.finish()


def attend(make):
    lines = [make(False, j) for j in range(LINES)]
    run(lines)
    fits = functools.reduce(jnp.minimum, [part for line in lines for part in line.fits])

    @pl.when(jnp.min(fits) < 0.5)
    def _():
        def again(j, carry):
            run([make(True, j)])
            return carry

        lax.fori_loop(0, LINES, again, 0)


def pick(first, left, right):
    if isinstance(first, bool):
        return left if first else right
    return jnp.where(first, left, right)


def row_kernel(
    cells, gain, qk_w, val_w, out_w, later_gain, last_gain, out, later_out, last_out, probs, turned
):
    later_out[...] = later_gain[...]
    last_out[...] = last_gain[...]

    def line(shift, j):
        def load():
            return cells[:, j].reshape(LINE, WIDTH).astype(jnp.float32)

        def store(done):
            for lanes in range(GROUPS):
                turned[lanes, pl.ds(j, LINE, stride=LINES), :] = done[:, lanes * HALF : (lanes + 1) * HALF]

        return Line(shift, load, store, gain, qk_w, val_w, out_w, probs)

    attend(line)
    n_row, n_col, deep = out.shape[:3]
    for lanes in range(GROUPS):
        here = slice(lanes * HALF, (lanes + 1) * HALF)
        blocks = turned[lanes].astype(jnp.bfloat16).reshape(n_col, n_row, deep, HALF)
        for r in range(n_row):
            out[r, :, :, here] = blocks[:, r]


def col_kernel(cells, gain, qk_w, val_w, out_w, out, probs):

    def line(shift, m):
        def load():
            tiles = cells[...].reshape(LINE // LINES, LINES * LINES, WIDTH)
            tiles = pick(m < 2, tiles[:, :8], tiles[:, 8:])
            tiles = tiles.astype(jnp.float32).reshape(LINE // 8, 2, 8, WIDTH)
            even, odd = tiles[:, 0], tiles[:, 1]
            first = m % 2 == 0
            even = pick(first, even, pltpu.roll(even, LINES, 1))
            odd = pick(first, pltpu.roll(odd, LINES, 1), odd)
            row = lax.broadcasted_iota(jnp.int32, even.shape, 1)
            return jnp.where(row < LINES, even, odd).reshape(LINE, WIDTH)

        def store(done):
            out[:, m] = done.astype(jnp.bfloat16).reshape(out.shape[0], out.shape[2], WIDTH)

        return Line(shift, load, store, gain, qk_w, val_w, out_w, probs)

    attend(line)


def mlp_kernel(blocks, gain, in_w, out_w, out, swap, done, sems):
    rows, cols = out.shape[:2]
    deep = rows // LINES
    cells = deep * cols
    to = lax.broadcasted_iota(jnp.int32, (cells, cells), 0)
    come = lax.broadcasted_iota(jnp.int32, (cells, cells), 1)
    moved = come == to % cols * deep + to // cols
    swap[...] = jnp.where(moved, 1.0, 0.0).astype(jnp.bfloat16)
    parts = [slice(part * deep, (part + 1) * deep) for part in range(LINES)]
    lines = [matmul(swap[...], blocks[:, :, here].reshape(cells, WIDTH)) for here in parts]
    normed = [layer_norm(line, gain[...]).astype(jnp.bfloat16) for line in lines]
    copies = []
    for part, here in enumerate(parts):
        for start in range(0, cells, BLOCK):
            pre = matmul(normed[part][start : start + BLOCK], in_w[...])
            inner = jnp.tanh(pre * (GELU_A + GELU_B * (pre * pre)))
            hidden = (pre * (0.5 + 0.5 * inner)).astype(jnp.bfloat16)
            result = lines[part][start : start + BLOCK] + matmul(hidden, out_w[...])
            first = part * deep + start // cols
            done[first : first + BLOCK // cols] = result.astype(jnp.bfloat16).reshape(
                BLOCK // cols, cols, WIDTH
            )
        copies.append(pltpu.make_async_copy(done.at[here], out.at[here], sems.at[part]))
        copies[-1].start()
    for copy in copies:
        copy.wait()


IN_VMEM = pl.BlockSpec(memory_space=pltpu.VMEM)
PARAMS = pltpu.CompilerParams(vmem_limit_bytes=40 * 2**20)


def bf16(*shape):
    return jax.ShapeDtypeStruct(shape, jnp.bfloat16)


def attend_scratch():
    return [pltpu.VMEM((HEADS, LINE, LINE), jnp.bfloat16)]


def row_attention(n_row, strips, gain, qk_w, val_w, out_w, *gains):
    n_col = strips.shape[0]
    return pl.pallas_call(
        row_kernel,
        in_specs=[IN_VMEM] * 7,
        out_specs=[IN_VMEM] * 3,
        out_shape=[bf16(n_row, n_col, LINES * LINES, WIDTH)]
        + [jax.ShapeDtypeStruct(later.shape, later.dtype) for later in gains],
        scratch_shapes=attend_scratch() + [pltpu.VMEM((GROUPS, LINES * LINE, HALF), jnp.float32)],
        compiler_params=PARAMS,
        name="row_attention",
    )(strips, gain, qk_w, val_w, out_w, *gains)


def col_attention(n_row, columns, *weights):
    return pl.pallas_call(
        col_kernel,
        in_specs=[IN_VMEM] * 5,
        out_specs=IN_VMEM,
        out_shape=bf16(n_row, LINES, LINE // n_row, WIDTH),
        scratch_shapes=attend_scratch(),
        compiler_params=PARAMS,
        name="col_attention",
    )(columns, *weights)


def mlp(cols, blocks, *weights):
    rows = blocks.shape[2]
    cells = rows // LINES * cols
    return pl.pallas_call(
        mlp_kernel,
        in_specs=[IN_VMEM] * 4,
        out_specs=pl.BlockSpec(memory_space=pl.ANY),
        out_shape=bf16(rows, cols, WIDTH),
        scratch_shapes=[
            pltpu.VMEM((cells, cells), jnp.bfloat16),
            pltpu.VMEM((rows, cols, WIDTH), jnp.bfloat16),
            pltpu.SemaphoreType.DMA((LINES,)),
        ],
        compiler_params=PARAMS,
        name="mlp",
    )(blocks, *weights)


def per_device(
    cells,
    row_gain,
    row_qk,
    row_value,
    row_out,
    col_gain,
    col_qk,
    col_value,
    col_out,
    mlp_gain,
    mlp_in,
    mlp_out,
):
    n_row = lax.axis_size("row")
    n_col = lax.axis_size("col")
    rows, cols, width = cells.shape
    row_gain, col_gain, mlp_gain = (g.reshape(1, width) for g in (row_gain, col_gain, mlp_gain))
    strips = lax.all_to_all(cells, "col", split_axis=0, concat_axis=0, tiled=True)
    strips = strips.reshape(n_col, LINES, cols, width)
    after_rows, col_gain, mlp_gain = row_attention(
        n_row, strips, row_gain, row_qk, row_value, row_out, col_gain, mlp_gain
    )
    columns = lax.all_to_all(
        after_rows.reshape(-1, width), ("row", "col"), split_axis=0, concat_axis=0, tiled=True
    )
    after_cols = col_attention(n_row, columns, col_gain, col_qk, col_value, col_out)
    blocks = lax.all_to_all(
        after_cols.reshape(-1, width), "row", split_axis=0, concat_axis=0, tiled=True
    )
    return mlp(cols, blocks.reshape(n_row, LINES, rows, width), mlp_gain, mlp_in, mlp_out)


def solution(mesh):
    in_specs = (P("row", "col", None), P(), P(), P(), P(), P(), P(), P(), P(), P(), P(), P())
    out_specs = P("row", "col", None)
    return jax.shard_map(
        per_device, mesh=mesh, in_specs=in_specs, out_specs=out_specs, check_vma=False
    )
```

profile of v0, /device:TPU:0, one launch (start us, length us, event | category | flops | bytes accessed | tf_op | source)
XLA Modules:
  0.0 115.4 jit_solution(524363081513059024)
XLA Ops:
  0.0 0.0 copy-start.7
  0.0 0.0 copy-start.6
  0.0 0.0 copy-start.3
  0.0 0.0 copy-start.9
  0.0 0.0 copy-start.10
  0.0 26.1 %all_to_all.25 = bf16[64,32,256]{2,1,0:T(8,128)(2,1)S(1)} all-to-all(bf16[64,32,256]{2,1,0:T(8,128)(2,1)} %param.12), channel_id=1, replica_groups=mesh['row'=8,'col'=16] {'col'}, dimensions={0} | all-to-all | bytes 2097152 | tf_op jit(solution)/shard_map/all_to_all | solution.py:302
  26.1 0.0 copy-start.8
  26.1 0.0 copy-done.7
  26.1 0.0 copy-done.6
  26.1 0.0 copy-done.3
  26.1 0.0 copy-done.9
  26.1 0.0 copy-done.10
  26.1 0.6 copy-done.8
  26.8 20.4 %row_attention.1 = (bf16[8,16,16,256]{3,2,1,0:T(8,128)(2,1)S(1)}, f32[1,256]{1,0:T(1,128)S(1)}, f32[1,256]{1,0:T(1,128)S(1)}) custom-call(bf16[16,4,32,256]{3,2,1,0:T(8,128)(2,1)S(1)} %bitcast.10, f32[1,256]{1,0:T(1,128)S(1)} %bitcast.13, bf16[256,512]{1,0:T(8,128)(2,1)S(1)} %copy-done.3, bf16[256,256]{1,0:T(8,128)(2,1)S(1)} %copy-done.6, ...), custom_call_target="tpu_custom_call" | custom-call | tf_op jit(solution)/shard_map/row_attention/pallas_call | solution.py:242
  47.2 0.0 copy-start.2
  47.2 0.0 copy-start.4
  47.2 0.0 copy-start.5
  47.3 23.5 %all_to_all.26 = bf16[128,16,256]{2,1,0:T(8,128)(2,1)S(1)} all-to-all(bf16[128,16,256]{2,1,0:T(8,128)(2,1)S(1)} %bitcast.12), channel_id=1, replica_groups=mesh['row'=8,'col'=16] {'row','col'}, dimensions={0} | all-to-all | bytes 2097152 | tf_op jit(solution)/shard_map/all_to_all | solution.py:307
  70.8 0.0 copy-done.2
  70.8 0.0 copy-done.4
  70.8 0.0 copy-done.5
  70.8 20.4 %col_attention.1 = bf16[8,4,64,256]{3,2,1,0:T(8,128)(2,1)S(1)} custom-call(bf16[2048,256]{1,0:T(8,128)(2,1)S(1)} %bitcast.8, f32[1,256]{1,0:T(1,128)S(1)} %get-tuple-element.9.gain, bf16[256,512]{1,0:T(8,128)(2,1)S(1)} %copy-done.2, bf16[256,256]{1,0:T(8,128)(2,1)S(1)} %copy-done.4, bf16[256,256]{1,0:T(8,128)(2,1)S(1)} %copy-done.5), custom_call_target="tpu_custom_call" | custom-call | tf_op jit(solution)/shard_map/col_attention/pallas_call | solution.py:255
  91.3 0.0 copy-start
  91.3 0.0 copy-start.1
  91.3 19.1 %all_to_all.27 = bf16[8,256,256]{2,1,0:T(8,128)(2,1)S(1)} all-to-all(bf16[8,256,256]{2,1,0:T(8,128)(2,1)S(1)} %bitcast.9), channel_id=1, replica_groups=mesh['row'=8,'col'=16] {'row'}, dimensions={0} | all-to-all | bytes 2097152 | tf_op jit(solution)/shard_map/all_to_all | solution.py:311
  110.3 0.0 copy-done
  110.3 0.0 copy-done.1
  110.3 4.9 %mlp.1 = bf16[64,32,256]{2,1,0:T(8,128)(2,1)} custom-call(bf16[8,4,64,256]{3,2,1,0:T(8,128)(2,1)S(1)} %bitcast.11, f32[1,256]{1,0:T(1,128)S(1)} %get-tuple-element.10.gain, bf16[256,1024]{1,0:T(8,128)(2,1)S(1)} %copy-done, bf16[1024,256]{1,0:T(8,128)(2,1)S(1)} %copy-done.1), custom_call_target="tpu_custom_call" | custom-call | tf_op jit(solution)/shard_map/mlp/pallas_call | solution.py:269
Async XLA Ops:
  0.0 26.1 %copy-start.7 = (bf16[256,256]{1,0:T(8,128)(2,1)S(1)}, bf16[256,256]{1,0:T(8,128)(2,1)}, u32[]{:S(2)}) copy-start(bf16[256,256]{1,0:T(8,128)(2,1)} %out_w.3) | copy-start | bytes 393220
  0.0 26.1 %copy-start.6 = (bf16[256,256]{1,0:T(8,128)(2,1)S(1)}, bf16[256,256]{1,0:T(8,128)(2,1)}, u32[]{:S(2)}) copy-start(bf16[256,256]{1,0:T(8,128)(2,1)} %val_w.2) | copy-start | bytes 393220
  0.0 26.1 %copy-start.3 = (bf16[256,512]{1,0:T(8,128)(2,1)S(1)}, bf16[256,512]{1,0:T(8,128)(2,1)}, u32[]{:S(2)}) copy-start(bf16[256,512]{1,0:T(8,128)(2,1)} %qk_w.2) | copy-start | bytes 786436
  0.0 26.1 %copy-start.9 = (f32[256]{0:T(256)S(1)}, f32[256]{0:T(256)}, u32[]{:S(2)}) copy-start(f32[256]{0:T(256)} %param.17) | copy-start | bytes 3076
  0.0 26.1 %copy-start.10 = (f32[256]{0:T(256)S(1)}, f32[256]{0:T(256)}, u32[]{:S(2)}) copy-start(f32[256]{0:T(256)} %param.21) | copy-start | bytes 3076
  26.1 0.7 copy-start.8
  47.2 23.6 %copy-start.2 = (bf16[256,512]{1,0:T(8,128)(2,1)S(1)}, bf16[256,512]{1,0:T(8,128)(2,1)}, u32[]{:S(2)}) copy-start(bf16[256,512]{1,0:T(8,128)(2,1)} %qk_w.3) | copy-start | bytes 786436
  47.2 23.6 %copy-start.4 = (bf16[256,256]{1,0:T(8,128)(2,1)S(1)}, bf16[256,256]{1,0:T(8,128)(2,1)}, u32[]{:S(2)}) copy-start(bf16[256,256]{1,0:T(8,128)(2,1)} %val_w.3) | copy-start | bytes 393220
  47.2 23.6 %copy-start.5 = (bf16[256,256]{1,0:T(8,128)(2,1)S(1)}, bf16[256,256]{1,0:T(8,128)(2,1)}, u32[]{:S(2)}) copy-start(bf16[256,256]{1,0:T(8,128)(2,1)} %out_w.4) | copy-start | bytes 393220
  91.3 19.1 %copy-start = (bf16[256,1024]{1,0:T(8,128)(2,1)S(1)}, bf16[256,1024]{1,0:T(8,128)(2,1)}, u32[]{:S(2)}) copy-start(bf16[256,1024]{1,0:T(8,128)(2,1)} %in_w.1) | copy-start | bytes 1572868
  91.3 19.1 %copy-start.1 = (bf16[1024,256]{1,0:T(8,128)(2,1)S(1)}, bf16[1024,256]{1,0:T(8,128)(2,1)}, u32[]{:S(2)}) copy-start(bf16[1024,256]{1,0:T(8,128)(2,1)} %out_w.5) | copy-start | bytes 1572868
where the time goes:
time: 116 us; the launch traced here: 115 us
  blocking collectives  68.7 us (59%)
  Pallas kernels  45.8 us (39%)
    all_to_all x1, blocking collectives, per_device(): lax.all_to_all(cells, 'col', split_axis=0, concat_axis=0, tiled=True)  26.1 us
    all_to_all x1, blocking collectives, per_device(): lax.all_to_all(after_rows.reshape(-1, width), ('row', 'col'), split_axis=...  23.5 us
    pallas_call x1, Pallas kernels, col_attention(): pl.pallas_call(col_kernel, in_specs=[IN_VMEM] * 5, out_specs=IN_VMEM, out...  20.4 us
    pallas_call x1, Pallas kernels, row_attention(): pl.pallas_call(row_kernel, in_specs=[IN_VMEM] * 7, out_specs=[IN_VMEM] *...  20.4 us
    all_to_all x1, blocking collectives, per_device(): lax.all_to_all(after_cols.reshape(-1, width), 'row', split_axis=0, concat...  19.1 us
    pallas_call x1, Pallas kernels, mlp(): pl.pallas_call(mlp_kernel, in_specs=[IN_VMEM] * 4, out_specs=pl.BlockSpec...  4.91 us

commit v1 on v0

--- a/solution.py
+++ b/solution.py
@@ -94,7 +94,7 @@
                 weight = total[HEAD : HEAD + 1]
                 fits = (weight >= LEAST) & (weight <= MOST)
                 self.fits.append(jnp.where(fits, 1.0, 0.0))
-            self.mixed.append((total[:HEAD] / total[HEAD : HEAD + 1]).astype(jnp.bfloat16))
+            self.mixed.append((total[:HEAD] * (1.0 / total[HEAD : HEAD + 1])).astype(jnp.bfloat16))
 
     def sum_chunks(self, group, head, values):
         chunks = range(0, LINE, self.chunk)
@@ -179,9 +179,8 @@
 
     def line(shift, m):
         def load():
-            tiles = cells[...].reshape(LINE // LINES, LINES * LINES, WIDTH)
-            tiles = pick(m < 2, tiles[:, :8], tiles[:, 8:])
-            tiles = tiles.astype(jnp.float32).reshape(LINE // 8, 2, 8, WIDTH)
+            tiles = cells[...].reshape(LINE // LINES, LINES * LINES, WIDTH).astype(jnp.float32)
+            tiles = pick(m < 2, tiles[:, :8], tiles[:, 8:]).reshape(LINE // 8, 2, 8, WIDTH)
             even, odd = tiles[:, 0], tiles[:, 1]
             first = m % 2 == 0
             even = pick(first, even, pltpu.roll(even, LINES, 1))
@@ -209,18 +208,20 @@
     lines = [matmul(swap[...], blocks[:, :, here].reshape(cells, WIDTH)) for here in parts]
     normed = [layer_norm(line, gain[...]).astype(jnp.bfloat16) for line in lines]
     copies = []
+
+    def widen(part):
+        pre = matmul(normed[part], in_w[...])
+        inner = jnp.tanh(pre * (GELU_A + GELU_B * (pre * pre)))
+        return (pre * (0.5 + 0.5 * inner)).astype(jnp.bfloat16)
+
+    hidden = widen(0)
     for part, here in enumerate(parts):
-        for start in range(0, cells, BLOCK):
-            pre = matmul(normed[part][start : start + BLOCK], in_w[...])
-            inner = jnp.tanh(pre * (GELU_A + GELU_B * (pre * pre)))
-            hidden = (pre * (0.5 + 0.5 * inner)).astype(jnp.bfloat16)
-            result = lines[part][start : start + BLOCK] + matmul(hidden, out_w[...])
-            first = part * deep + start // cols
-            done[first : first + BLOCK // cols] = result.astype(jnp.bfloat16).reshape(
-                BLOCK // cols, cols, WIDTH
-            )
+        later = widen(part + 1) if part + 1 < LINES else None
+        result = lines[part] + matmul(hidden, out_w[...])
+        done[here] = result.astype(jnp.bfloat16).reshape(deep, cols, WIDTH)
         copies.append(pltpu.make_async_copy(done.at[here], out.at[here], sems.at[part]))
         copies[-1].start()
+        hidden = later
     for copy in copies:
         copy.wait()
 

time: 116 us -> 116 us (level)
  no operation moved by 1% of the time
where the time goes in v1:
time: 116 us
  blocking collectives  68.7 us (59%)
  Pallas kernels  46.1 us (40%)
    all_to_all x1, blocking collectives, per_device(): lax.all_to_all(cells, 'col', split_axis=0, concat_axis=0, tiled=True)  26.1 us
    all_to_all x1, blocking collectives, per_device(): lax.all_to_all(after_rows.reshape(-1, width), ('row', 'col'), split_axis=...  23.6 us
    pallas_call x1, Pallas kernels, col_attention(): pl.pallas_call(col_kernel, in_specs=[IN_VMEM] * 5, out_specs=IN_VMEM, out...  21 us
    pallas_call x1, Pallas kernels, row_attention(): pl.pallas_call(row_kernel, in_specs=[IN_VMEM] * 7, out_specs=[IN_VMEM] *...  20.4 us
    all_to_all x1, blocking collectives, per_device(): lax.all_to_all(after_cols.reshape(-1, width), 'row', split_axis=0, concat...  19 us
    pallas_call x1, Pallas kernels, mlp(): pl.pallas_call(mlp_kernel, in_specs=[IN_VMEM] * 4, out_specs=pl.BlockSpec...  4.76 us

profile of v1, /device:TPU:0, one launch (start us, length us, event | category | flops | bytes accessed | tf_op | source)
XLA Modules:
  0.0 115.7 jit_solution(12204164963879403769)
XLA Ops:
  0.0 0.0 copy-start.7
  0.0 0.0 copy-start.6
  0.0 0.0 copy-start.3
  0.0 0.0 copy-start.9
  0.0 0.0 copy-start.10
  0.0 26.1 %all_to_all.25 = bf16[64,32,256]{2,1,0:T(8,128)(2,1)S(1)} all-to-all(bf16[64,32,256]{2,1,0:T(8,128)(2,1)} %param.12), channel_id=1, replica_groups=mesh['row'=8,'col'=16] {'col'}, dimensions={0} | all-to-all | bytes 2097152 | tf_op jit(solution)/shard_map/all_to_all | solution.py:303
  26.1 0.0 copy-start.8
  26.1 0.0 copy-done.7
  26.1 0.0 copy-done.6
  26.1 0.0 copy-done.3
  26.1 0.0 copy-done.9
  26.1 0.0 copy-done.10
  26.1 0.6 copy-done.8
  26.8 20.4 %row_attention.1 = (bf16[8,16,16,256]{3,2,1,0:T(8,128)(2,1)S(1)}, f32[1,256]{1,0:T(1,128)S(1)}, f32[1,256]{1,0:T(1,128)S(1)}) custom-call(bf16[16,4,32,256]{3,2,1,0:T(8,128)(2,1)S(1)} %bitcast.10, f32[1,256]{1,0:T(1,128)S(1)} %bitcast.13, bf16[256,512]{1,0:T(8,128)(2,1)S(1)} %copy-done.3, bf16[256,256]{1,0:T(8,128)(2,1)S(1)} %copy-done.6, ...), custom_call_target="tpu_custom_call" | custom-call | tf_op jit(solution)/shard_map/row_attention/pallas_call | solution.py:243
  47.2 0.0 copy-start.2
  47.2 0.0 copy-start.4
  47.2 0.0 copy-start.5
  47.2 23.6 %all_to_all.26 = bf16[128,16,256]{2,1,0:T(8,128)(2,1)S(1)} all-to-all(bf16[128,16,256]{2,1,0:T(8,128)(2,1)S(1)} %bitcast.12), channel_id=1, replica_groups=mesh['row'=8,'col'=16] {'row','col'}, dimensions={0} | all-to-all | bytes 2097152 | tf_op jit(solution)/shard_map/all_to_all | solution.py:308
  70.8 0.0 copy-done.2
  70.8 0.0 copy-done.4
  70.8 0.0 copy-done.5
  70.8 21.0 %col_attention.1 = bf16[8,4,64,256]{3,2,1,0:T(8,128)(2,1)S(1)} custom-call(bf16[2048,256]{1,0:T(8,128)(2,1)S(1)} %bitcast.8, f32[1,256]{1,0:T(1,128)S(1)} %get-tuple-element.9.gain, bf16[256,512]{1,0:T(8,128)(2,1)S(1)} %copy-done.2, bf16[256,256]{1,0:T(8,128)(2,1)S(1)} %copy-done.4, bf16[256,256]{1,0:T(8,128)(2,1)S(1)} %copy-done.5), custom_call_target="tpu_custom_call" | custom-call | tf_op jit(solution)/shard_map/col_attention/pallas_call | solution.py:256
  91.7 0.0 copy-start
  91.8 0.0 copy-start.1
  91.8 19.0 %all_to_all.27 = bf16[8,256,256]{2,1,0:T(8,128)(2,1)S(1)} all-to-all(bf16[8,256,256]{2,1,0:T(8,128)(2,1)S(1)} %bitcast.9), channel_id=1, replica_groups=mesh['row'=8,'col'=16] {'row'}, dimensions={0} | all-to-all | bytes 2097152 | tf_op jit(solution)/shard_map/all_to_all | solution.py:312
  110.8 0.0 copy-done
  110.8 0.0 copy-done.1
  110.8 4.8 %mlp.1 = bf16[64,32,256]{2,1,0:T(8,128)(2,1)} custom-call(bf16[8,4,64,256]{3,2,1,0:T(8,128)(2,1)S(1)} %bitcast.11, f32[1,256]{1,0:T(1,128)S(1)} %get-tuple-element.10.gain, bf16[256,1024]{1,0:T(8,128)(2,1)S(1)} %copy-done, bf16[1024,256]{1,0:T(8,128)(2,1)S(1)} %copy-done.1), custom_call_target="tpu_custom_call" | custom-call | tf_op jit(solution)/shard_map/mlp/pallas_call | solution.py:270
Async XLA Ops:
  0.0 26.1 %copy-start.7 = (bf16[256,256]{1,0:T(8,128)(2,1)S(1)}, bf16[256,256]{1,0:T(8,128)(2,1)}, u32[]{:S(2)}) copy-start(bf16[256,256]{1,0:T(8,128)(2,1)} %out_w.3) | copy-start | bytes 393220
  0.0 26.1 %copy-start.6 = (bf16[256,256]{1,0:T(8,128)(2,1)S(1)}, bf16[256,256]{1,0:T(8,128)(2,1)}, u32[]{:S(2)}) copy-start(bf16[256,256]{1,0:T(8,128)(2,1)} %val_w.2) | copy-start | bytes 393220
  0.0 26.1 %copy-start.3 = (bf16[256,512]{1,0:T(8,128)(2,1)S(1)}, bf16[256,512]{1,0:T(8,128)(2,1)}, u32[]{:S(2)}) copy-start(bf16[256,512]{1,0:T(8,128)(2,1)} %qk_w.2) | copy-start | bytes 786436
  0.0 26.1 %copy-start.9 = (f32[256]{0:T(256)S(1)}, f32[256]{0:T(256)}, u32[]{:S(2)}) copy-start(f32[256]{0:T(256)} %param.17) | copy-start | bytes 3076
  0.0 26.1 %copy-start.10 = (f32[256]{0:T(256)S(1)}, f32[256]{0:T(256)}, u32[]{:S(2)}) copy-start(f32[256]{0:T(256)} %param.21) | copy-start | bytes 3076
  26.1 0.7 copy-start.8
  47.2 23.6 %copy-start.2 = (bf16[256,512]{1,0:T(8,128)(2,1)S(1)}, bf16[256,512]{1,0:T(8,128)(2,1)}, u32[]{:S(2)}) copy-start(bf16[256,512]{1,0:T(8,128)(2,1)} %qk_w.3) | copy-start | bytes 786436
  47.2 23.6 %copy-start.4 = (bf16[256,256]{1,0:T(8,128)(2,1)S(1)}, bf16[256,256]{1,0:T(8,128)(2,1)}, u32[]{:S(2)}) copy-start(bf16[256,256]{1,0:T(8,128)(2,1)} %val_w.3) | copy-start | bytes 393220
  47.2 23.6 %copy-start.5 = (bf16[256,256]{1,0:T(8,128)(2,1)S(1)}, bf16[256,256]{1,0:T(8,128)(2,1)}, u32[]{:S(2)}) copy-start(bf16[256,256]{1,0:T(8,128)(2,1)} %out_w.4) | copy-start | bytes 393220
  91.7 19.0 %copy-start = (bf16[256,1024]{1,0:T(8,128)(2,1)S(1)}, bf16[256,1024]{1,0:T(8,128)(2,1)}, u32[]{:S(2)}) copy-start(bf16[256,1024]{1,0:T(8,128)(2,1)} %in_w.1) | copy-start | bytes 1572868
  91.8 19.0 %copy-start.1 = (bf16[1024,256]{1,0:T(8,128)(2,1)S(1)}, bf16[1024,256]{1,0:T(8,128)(2,1)}, u32[]{:S(2)}) copy-start(bf16[1024,256]{1,0:T(8,128)(2,1)} %out_w.5) | copy-start | bytes 1572868

commit v2 on v1

--- a/solution.py
+++ b/solution.py
@@ -150,11 +150,10 @@
     return jnp.where(first, left, right)
 
 
-def row_kernel(
-    cells, gain, qk_w, val_w, out_w, later_gain, last_gain, out, later_out, last_out, probs, turned
-):
-    later_out[...] = later_gain[...]
-    last_out[...] = last_gain[...]
+def row_kernel(cells, gains, qk_w, val_w, out_w, out, later_out, last_out, probs, turned):
+    gain = gains.at[0:1]
+    later_out[...] = gains[1:2]
+    last_out[...] = gains[2:3]
 
     def line(shift, j):
         def load():
@@ -238,18 +237,18 @@
     return [pltpu.VMEM((HEADS, LINE, LINE), jnp.bfloat16)]
 
 
-def row_attention(n_row, strips, gain, qk_w, val_w, out_w, *gains):
+def row_attention(n_row, strips, gains, qk_w, val_w, out_w):
     n_col = strips.shape[0]
     return pl.pallas_call(
         row_kernel,
-        in_specs=[IN_VMEM] * 7,
+        in_specs=[IN_VMEM] * 5,
         out_specs=[IN_VMEM] * 3,
         out_shape=[bf16(n_row, n_col, LINES * LINES, WIDTH)]
-        + [jax.ShapeDtypeStruct(later.shape, later.dtype) for later in gains],
+        + [jax.ShapeDtypeStruct((1, WIDTH), jnp.float32)] * 2,
         scratch_shapes=attend_scratch() + [pltpu.VMEM((GROUPS, LINES * LINE, HALF), jnp.float32)],
         compiler_params=PARAMS,
         name="row_attention",
-    )(strips, gain, qk_w, val_w, out_w, *gains)
+    )(strips, gains, qk_w, val_w, out_w)
 
 
 def col_attention(n_row, columns, *weights):
@@ -299,12 +298,10 @@
     n_row = lax.axis_size("row")
     n_col = lax.axis_size("col")
     rows, cols, width = cells.shape
-    row_gain, col_gain, mlp_gain = (g.reshape(1, width) for g in (row_gain, col_gain, mlp_gain))
+    gains = jnp.stack([row_gain, col_gain, mlp_gain])
     strips = lax.all_to_all(cells, "col", split_axis=0, concat_axis=0, tiled=True)
     strips = strips.reshape(n_col, LINES, cols, width)
-    after_rows, col_gain, mlp_gain = row_attention(
-        n_row, strips, row_gain, row_qk, row_value, row_out, col_gain, mlp_gain
-    )
+    after_rows, col_gain, mlp_gain = row_attention(n_row, strips, gains, row_qk, row_value, row_out)
     columns = lax.all_to_all(
         after_rows.reshape(-1, width), ("row", "col"), split_axis=0, concat_axis=0, tiled=True
     )

time: 116 us -> 115 us (level)
  blocking collectives: 68.7 us -> 42.6 us
  waiting for transfers between devices: 0 us -> 17.3 us
  starting transfers between devices: 0 us -> 8.12 us
    all_to_all x1 -> x0, blocking collectives: 26.1 us -> none  [per_device(): lax.all_to_all(cells, 'col', split_axis=0, concat_axis=0, tiled=True)]
    all_to_all x0 -> x1, waiting for transfers between devices: none -> 17.3 us  [per_device(): lax.all_to_all(cells, 'col', split_axis=0, concat_axis=0, tiled=True)]
    all_to_all x0 -> x1, starting transfers between devices: none -> 8.12 us  [per_device(): lax.all_to_all(cells, 'col', split_axis=0, concat_axis=0, tiled=True)]
  transfers between devices with their start and end apart: 0 -> 1, of which waited for: 0 -> 1; matrix products, arithmetic and copies ran while one was open for 0% -> 0% of each run, Pallas kernels for 0% -> 0%
where the time goes in v2:
time: 115 us
  Pallas kernels  46 us (40%)
  blocking collectives  42.6 us (37%)
  waiting for transfers between devices  17.3 us (15%)
  starting transfers between devices  8.12 us (7%)
    all_to_all x1, blocking collectives, per_device(): lax.all_to_all(after_rows.reshape(-1, width), ('row', 'col'), split_axis=...  23.6 us
    pallas_call x1, Pallas kernels, col_attention(): pl.pallas_call(col_kernel, in_specs=[IN_VMEM] * 5, out_specs=IN_VMEM, out...  20.9 us
    pallas_call x1, Pallas kernels, row_attention(): pl.pallas_call(row_kernel, in_specs=[IN_VMEM] * 5, out_specs=[IN_VMEM] *...  20.3 us
    all_to_all x1, blocking collectives, per_device(): lax.all_to_all(after_cols.reshape(-1, width), 'row', split_axis=0, concat...  19 us
    all_to_all x1, waiting for transfers between devices, per_device(): lax.all_to_all(cells, 'col', split_axis=0, concat_axis=0, tiled=True)  17.3 us
    all_to_all x1, starting transfers between devices, per_device(): lax.all_to_all(cells, 'col', split_axis=0, concat_axis=0, tiled=True)  8.12 us
    pallas_call x1, Pallas kernels, mlp(): pl.pallas_call(mlp_kernel, in_specs=[IN_VMEM] * 4, out_specs=pl.BlockSpec...  4.74 us
  transfers between devices with their start and end apart: 1, of which 1 were waited for; matrix products, arithmetic and copies ran while one was open for 0% of the time, Pallas kernels for 0%

profile of v2, /device:TPU:0, one launch (start us, length us, event | category | flops | bytes accessed | tf_op | source)
XLA Modules:
  0.0 115.0 jit_solution(174559647580411252)
XLA Ops:
  0.0 0.0 copy-start.5
  0.0 0.0 copy-start.4
  0.0 0.0 copy-start.3
  0.0 0.0 copy-start.9
  0.0 0.0 copy-start.10
  0.0 8.1 %all-to-all-start = ((bf16[64,32,256]{2,1,0:T(8,128)(2,1)}), bf16[64,32,256]{2,1,0:T(8,128)(2,1)S(1)}, u32[]{:S(2)}, u32[]{:S(2)}) async-start(bf16[64,32,256]{2,1,0:T(8,128)(2,1)} %param.12), calls=%async_computation | async-start | bytes 2097152 | tf_op jit(solution)/shard_map/all_to_all | solution.py:302
  8.1 0.0 copy-start.8
  8.2 0.0 copy-done.9
  8.2 0.0 copy-done.10
  8.2 0.7 copy-done.8
  8.8 17.3 %all-to-all-done = bf16[64,32,256]{2,1,0:T(8,128)(2,1)S(1)} async-done(((bf16[64,32,256]{2,1,0:T(8,128)(2,1)}), bf16[64,32,256]{2,1,0:T(8,128)(2,1)S(1)}, u32[]{:S(2)}, u32[]{:S(2)}) %all-to-all-start) | async-done | bytes 1048608 | tf_op jit(solution)/shard_map/all_to_all | solution.py:302
  26.2 0.0 copy-done.5
  26.2 0.0 copy-done.4
  26.2 0.0 copy-done.3
  26.2 20.3 %row_attention.1 = (bf16[8,16,16,256]{3,2,1,0:T(8,128)(2,1)S(1)}, f32[1,256]{1,0:T(1,128)S(1)}, f32[1,256]{1,0:T(1,128)S(1)}) custom-call(bf16[16,4,32,256]{3,2,1,0:T(8,128)(2,1)S(1)} %bitcast.10, f32[3,256]{1,0:T(4,128)S(1)} %pad_maximum_fusion.gains, bf16[256,512]{1,0:T(8,128)(2,1)S(1)} %copy-done.3, bf16[256,256]{1,0:T(8,128)(2,1)S(1)} %copy-done.4, ...), custom_call_target="tpu_custom_call" | custom-call | tf_op jit(solution)/shard_map/row_attention/pallas_call | solution.py:242
  46.5 0.0 copy-start.2
  46.5 0.0 copy-start.6
  46.5 0.0 copy-start.7
  46.6 23.6 %all_to_all.25 = bf16[128,16,256]{2,1,0:T(8,128)(2,1)S(1)} all-to-all(bf16[128,16,256]{2,1,0:T(8,128)(2,1)S(1)} %bitcast.12), channel_id=1, replica_groups=mesh['row'=8,'col'=16] {'row','col'}, dimensions={0} | all-to-all | bytes 2097152 | tf_op jit(solution)/shard_map/all_to_all | solution.py:305
  70.2 0.0 copy-done.2
  70.2 0.0 copy-done.6
  70.2 0.0 copy-done.7
  70.2 20.9 %col_attention.1 = bf16[8,4,64,256]{3,2,1,0:T(8,128)(2,1)S(1)} custom-call(bf16[2048,256]{1,0:T(8,128)(2,1)S(1)} %bitcast.8, f32[1,256]{1,0:T(1,128)S(1)} %get-tuple-element.9.gain, bf16[256,512]{1,0:T(8,128)(2,1)S(1)} %copy-done.2, bf16[256,256]{1,0:T(8,128)(2,1)S(1)} %copy-done.6, bf16[256,256]{1,0:T(8,128)(2,1)S(1)} %copy-done.7), custom_call_target="tpu_custom_call" | custom-call | tf_op jit(solution)/shard_map/col_attention/pallas_call | solution.py:255
  91.1 0.0 copy-start
  91.1 0.0 copy-start.1
  91.1 19.0 %all_to_all.26 = bf16[8,256,256]{2,1,0:T(8,128)(2,1)S(1)} all-to-all(bf16[8,256,256]{2,1,0:T(8,128)(2,1)S(1)} %bitcast.9), channel_id=1, replica_groups=mesh['row'=8,'col'=16] {'row'}, dimensions={0} | all-to-all | bytes 2097152 | tf_op jit(solution)/shard_map/all_to_all | solution.py:309
  110.1 0.0 copy-done
  110.1 0.0 copy-done.1
  110.1 4.7 %mlp.1 = bf16[64,32,256]{2,1,0:T(8,128)(2,1)} custom-call(bf16[8,4,64,256]{3,2,1,0:T(8,128)(2,1)S(1)} %bitcast.11, f32[1,256]{1,0:T(1,128)S(1)} %get-tuple-element.10.gain, bf16[256,1024]{1,0:T(8,128)(2,1)S(1)} %copy-done, bf16[1024,256]{1,0:T(8,128)(2,1)S(1)} %copy-done.1), custom_call_target="tpu_custom_call" | custom-call | tf_op jit(solution)/shard_map/mlp/pallas_call | solution.py:269
  (1 shorter events, 0.0 us)
Async XLA Ops:
  0.0 26.2 %copy-start.5 = (bf16[256,256]{1,0:T(8,128)(2,1)S(1)}, bf16[256,256]{1,0:T(8,128)(2,1)}, u32[]{:S(2)}) copy-start(bf16[256,256]{1,0:T(8,128)(2,1)} %out_w.3) | copy-start | bytes 393220
  0.0 26.2 %copy-start.4 = (bf16[256,256]{1,0:T(8,128)(2,1)S(1)}, bf16[256,256]{1,0:T(8,128)(2,1)}, u32[]{:S(2)}) copy-start(bf16[256,256]{1,0:T(8,128)(2,1)} %val_w.2) | copy-start | bytes 393220
  0.0 26.2 %copy-start.3 = (bf16[256,512]{1,0:T(8,128)(2,1)S(1)}, bf16[256,512]{1,0:T(8,128)(2,1)}, u32[]{:S(2)}) copy-start(bf16[256,512]{1,0:T(8,128)(2,1)} %qk_w.2) | copy-start | bytes 786436
  0.0 8.1 %copy-start.9 = (f32[256]{0:T(256)S(1)}, f32[256]{0:T(256)}, u32[]{:S(2)}) copy-start(f32[256]{0:T(256)} %param.17) | copy-start | bytes 3076
  0.0 8.2 %copy-start.10 = (f32[256]{0:T(256)S(1)}, f32[256]{0:T(256)}, u32[]{:S(2)}) copy-start(f32[256]{0:T(256)} %param.13) | copy-start | bytes 3076
  0.0 26.2 %all-to-all-start = ((bf16[64,32,256]{2,1,0:T(8,128)(2,1)}), bf16[64,32,256]{2,1,0:T(8,128)(2,1)S(1)}, u32[]{:S(2)}, u32[]{:S(2)}) async-start(bf16[64,32,256]{2,1,0:T(8,128)(2,1)} %param.12), calls=%async_computation | async-start | bytes 2097152 | tf_op jit(solution)/shard_map/all_to_all | solution.py:302
  8.1 0.7 copy-start.8
  46.5 23.7 %copy-start.2 = (bf16[256,512]{1,0:T(8,128)(2,1)S(1)}, bf16[256,512]{1,0:T(8,128)(2,1)}, u32[]{:S(2)}) copy-start(bf16[256,512]{1,0:T(8,128)(2,1)} %qk_w.3) | copy-start | bytes 786436
  46.5 23.6 %copy-start.6 = (bf16[256,256]{1,0:T(8,128)(2,1)S(1)}, bf16[256,256]{1,0:T(8,128)(2,1)}, u32[]{:S(2)}) copy-start(bf16[256,256]{1,0:T(8,128)(2,1)} %val_w.3) | copy-start | bytes 393220
  46.5 23.6 %copy-start.7 = (bf16[256,256]{1,0:T(8,128)(2,1)S(1)}, bf16[256,256]{1,0:T(8,128)(2,1)}, u32[]{:S(2)}) copy-start(bf16[256,256]{1,0:T(8,128)(2,1)} %out_w.4) | copy-start | bytes 393220
  91.1 19.0 %copy-start = (bf16[256,1024]{1,0:T(8,128)(2,1)S(1)}, bf16[256,1024]{1,0:T(8,128)(2,1)}, u32[]{:S(2)}) copy-start(bf16[256,1024]{1,0:T(8,128)(2,1)} %in_w.1) | copy-start | bytes 1572868
  91.1 19.0 %copy-start.1 = (bf16[1024,256]{1,0:T(8,128)(2,1)S(1)}, bf16[1024,256]{1,0:T(8,128)(2,1)}, u32[]{:S(2)}) copy-start(bf16[1024,256]{1,0:T(8,128)(2,1)} %out_w.5) | copy-start | bytes 1572868
